TPU v7x, 32 devices: a whole 2x2x4 slice. The times are simulated.
32 devices in a mesh: dp: 8 (over z, x), fsdp: 4 (over y, core).
Axes of the slice: x: 2, y: 2, z: 4, core: 2. Of those that a mesh axis runs over, the one named last changes fastest.
Arguments:
- chars: int32 [2, 1024, 6], P(None, ('dp', 'fsdp')), may hold values from 0 to 274
- resets: int32 [2, 1024, 6], P(None, ('dp', 'fsdp')), may hold values 0 or 1
- targets: int32 [2, 1024, 6], P(None, ('dp', 'fsdp')), may hold values from 0 to 274
- embed: bfloat16 [275, 100], replicated, may hold values from -6 to 6
- w_in: bfloat16 [100, 8192], P(None, ('dp', 'fsdp')), may hold values from -0.625 to 0.625
- bias_in: bfloat16 [8192], P(('dp', 'fsdp')), may hold values from -3 to 3
- w_rec: bfloat16 [2048, 8192], P(('dp', 'fsdp')), may hold values from -0.125 to 0.125
- w_dec: bfloat16 [2048, 275], P(('dp', 'fsdp')), may hold values from -0.59765625 to 0.59765625
- bias_dec: bfloat16 [275], replicated, may hold values from -6 to 6
Outputs:
- loss: float32 [], replicated
- hidden: bfloat16 [2, 1024, 6, 2048], P(None, ('dp', 'fsdp'))
- grad_embed: float32 [275, 100], replicated
- grad_w_in: float32 [100, 8192], P(None, ('dp', 'fsdp'))
- grad_bias_in: float32 [8192], P(('dp', 'fsdp'))
- grad_w_rec: float32 [2048, 8192], P(('dp', 'fsdp'))
- grad_w_dec: float32 [2048, 275], P(('dp', 'fsdp'))
- grad_bias_dec: float32 [275], replicated
All inputs are finite; a program needn't handle non-finite values. No bound on the sum of `resets` on one device may be relied on, other than what follows from the above.
Results may differ from a plain program's by a relative error of at most 0.0027.
Values may be sent and summed in bfloat16 or wider, within the bound.
A program may use at most 192 MiB of HBM per device.

v0:
```python
import jax
import jax.numpy as jnp
from jax import lax
from jax.sharding import PartitionSpec as P


def dot_plain(left, right):
    return jnp.dot(left, right, preferred_element_type=jnp.float32)


def dot_right_t(left, right):
    return lax.dot_general(
        left, right, (((1,), (1,)), ((), ())), preferred_element_type=jnp.float32
    )


def dot_left_t(left, right):
    return lax.dot_general(
        left, right, (((0,), (0,)), ((), ())), preferred_element_type=jnp.float32
    )


def lstm_forward(weights, embed, bias_dec, ids, marks, goals):
    w_rec, w_dec, w_in, bias_in = weights
    count, steps = ids.shape
    width = w_rec.shape[0]
    letters = jnp.arange(embed.shape[0], dtype=jnp.int32)
    onehot = (ids.T.reshape(-1)[:, None] == letters[None, :]).astype(jnp.bfloat16)
    feature = dot_plain(onehot, embed).astype(jnp.bfloat16)
    drives = (dot_plain(feature, w_in) + bias_in.astype(jnp.float32)).reshape(steps, count, -1)
    keeps = (1 - marks.T).astype(jnp.float32)[:, :, None]

    def advance(state, slot):
        hidden_now, cell = state
        drive, keep_now = slot
        prev_hidden = hidden_now * keep_now.astype(jnp.bfloat16)
        prev_cell = cell * keep_now
        pre = drive + dot_plain(prev_hidden, w_rec)
        gin, gforget, gcand, gout = jnp.split(pre, 4, axis=1)
        cell_new = jax.nn.sigmoid(gforget) * prev_cell + jax.nn.sigmoid(gin) * jnp.tanh(gcand)
        hid_new = (jax.nn.sigmoid(gout) * jnp.tanh(cell_new)).astype(jnp.bfloat16)
        return ((hid_new, cell_new), (pre, prev_hidden, prev_cell, cell_new, hid_new))

    start = (jnp.zeros((count, width), jnp.bfloat16), jnp.zeros((count, width), jnp.float32))
    state, saved = lax.scan(advance, start, (drives, keeps))
    pres, prev_hiddens, prev_cells, cells, hiddens = saved
    flat_hidden = hiddens.reshape(steps * count, width)
    logits = dot_plain(flat_hidden, w_dec) + bias_dec.astype(jnp.float32)
    top = jnp.max(logits, axis=1, keepdims=True)
    shifted = jnp.exp(logits - top)
    summed = jnp.sum(shifted, axis=1, keepdims=True)
    goal_hot = (goals.T.reshape(-1)[:, None] == letters[None, :]).astype(jnp.float32)
    loss_part = jnp.sum(top[:, 0] + jnp.log(summed[:, 0])) - jnp.sum(goal_hot * logits)
    d_logits = (shifted / summed - goal_hot).astype(jnp.bfloat16)
    kept = (pres, prev_hiddens, prev_cells, cells, keeps, flat_hidden, d_logits, feature, onehot)
    return (kept, loss_part, jnp.transpose(hiddens, (1, 0, 2)))


def lstm_backward(weights, kept):
    w_rec, w_dec, w_in, bias_in = weights
    pres, prev_hiddens, prev_cells, cells, keeps, flat_hidden, d_logits, feature, onehot = kept
    steps, count, width = cells.shape
    from_dec = dot_right_t(d_logits, w_dec).reshape(steps, count, width)

    def retreat(carry, slot):
        grad_h, grad_c = carry
        pre, prev_cell, cell, extra, keep_now = slot
        gin, gforget, gcand, gout = jnp.split(pre, 4, axis=1)
        sig_in = jax.nn.sigmoid(gin)
        sig_forget = jax.nn.sigmoid(gforget)
        sig_out = jax.nn.sigmoid(gout)
        tan_cand = jnp.tanh(gcand)
        tan_cell = jnp.tanh(cell)
        grad_hid = extra + grad_h
        grad_out = grad_hid * tan_cell
        grad_cell = grad_c + grad_hid * sig_out * (1.0 - tan_cell * tan_cell)
        d_pre = jnp.concatenate(
            [
                grad_cell * tan_cand * sig_in * (1.0 - sig_in),
                grad_cell * prev_cell * sig_forget * (1.0 - sig_forget),
                grad_cell * sig_in * (1.0 - tan_cand * tan_cand),
                grad_out * sig_out * (1.0 - sig_out),
            ],
            axis=1,
        ).astype(jnp.bfloat16)
        back_h = dot_right_t(d_pre, w_rec) * keep_now
        back_c = grad_cell * sig_forget * keep_now
        return ((back_h, back_c), d_pre)

    start = (jnp.zeros((count, width), jnp.float32), jnp.zeros((count, width), jnp.float32))
    state, d_pres = lax.scan(
        retreat, start, (pres, prev_cells, cells, from_dec, keeps), reverse=True
    )
    flat_pre = d_pres.reshape(steps * count, -1)
    grad_dec = dot_left_t(flat_hidden, d_logits)
    grad_in = dot_left_t(feature, flat_pre)
    grad_bias = jnp.sum(flat_pre.astype(jnp.float32), axis=0)
    grad_feature = dot_right_t(flat_pre, w_in)
    grad_table = lax.dot_general(
        onehot.astype(jnp.float32),
        grad_feature,
        (((0,), (0,)), ((), ())),
        precision=lax.Precision.HIGHEST,
        preferred_element_type=jnp.float32,
    )
    grad_bias_out = jnp.sum(d_logits.astype(jnp.float32), axis=0)
    flat_prev = prev_hiddens.reshape(steps * count, width)
    return (grad_dec, grad_in, grad_bias, grad_table, grad_bias_out, flat_prev, flat_pre)


def per_device(chars, resets, targets, embed, w_in, bias_in, w_rec, w_dec, bias_dec):
    micro, count, steps = chars.shape
    everyone = lax.axis_size(("dp", "fsdp"))
    sums = None
    prev_list = []
    pre_list = []
    hidden_list = []
    for index in range(micro):
        forward_set = (
            lax.all_gather(w_rec, ("dp", "fsdp"), axis=0, tiled=True),
            lax.all_gather(w_dec, ("dp", "fsdp"), axis=0, tiled=True),
            lax.all_gather(w_in, ("dp", "fsdp"), axis=1, tiled=True),
            lax.all_gather(bias_in, ("dp", "fsdp"), axis=0, tiled=True),
        )
        kept, loss_part, hiddens = lstm_forward(
            forward_set, embed, bias_dec, chars[index], resets[index], targets[index]
        )
        backward_set = (
            lax.all_gather(w_rec, ("dp", "fsdp"), axis=0, tiled=True),
            lax.all_gather(w_dec, ("dp", "fsdp"), axis=0, tiled=True),
            lax.all_gather(w_in, ("dp", "fsdp"), axis=1, tiled=True),
            lax.all_gather(bias_in, ("dp", "fsdp"), axis=0, tiled=True),
        )
        grad_dec, grad_in, grad_bias, grad_table, grad_bias_out, flat_prev, flat_pre = (
            lstm_backward(backward_set, kept)
        )
        pieces = (grad_dec, grad_in, grad_bias, grad_table, grad_bias_out, loss_part)
        if sums is None:
            sums = pieces
        else:
            sums = tuple((first + second for first, second in zip(sums, pieces)))
        prev_list.append(flat_prev)
        pre_list.append(flat_pre)
        hidden_list.append(hiddens)
    prev_all = jnp.concatenate(prev_list, axis=0)
    pre_all = jnp.concatenate(pre_list, axis=0)
    grad_w_rec = lax.psum_scatter(
        dot_left_t(prev_all, pre_all), ("dp", "fsdp"), scatter_dimension=0, tiled=True
    )
    grad_w_dec, grad_w_in, grad_bias_in = (
        lax.psum_scatter(sums[0], ("dp", "fsdp"), scatter_dimension=0, tiled=True),
        lax.psum_scatter(sums[1], ("dp", "fsdp"), scatter_dimension=1, tiled=True),
        lax.psum_scatter(sums[2], ("dp", "fsdp"), scatter_dimension=0, tiled=True),
    )
    grad_embed, grad_bias_dec, total = lax.psum((sums[3], sums[4], sums[5]), ("dp", "fsdp"))
    loss = total / (micro * count * steps * everyone)
    hidden = jnp.stack(hidden_list, axis=0)
    return (
        loss,
        hidden,
        grad_embed,
        grad_w_in,
        grad_bias_in,
        grad_w_rec,
        grad_w_dec,
        grad_bias_dec,
    )


def solution(mesh):
    return jax.shard_map(
        per_device,
        mesh=mesh,
        in_specs=(
            P(None, ("dp", "fsdp"), None),
            P(None, ("dp", "fsdp"), None),
            P(None, ("dp", "fsdp"), None),
            P(),
            P(None, ("dp", "fsdp")),
            P(("dp", "fsdp")),
            P(("dp", "fsdp"), None),
            P(("dp", "fsdp"), None),
            P(),
        ),
        out_specs=(
            P(),
            P(None, ("dp", "fsdp"), None, None),
            P(),
            P(None, ("dp", "fsdp")),
            P(("dp", "fsdp")),
            P(("dp", "fsdp"), None),
            P(("dp", "fsdp"), None),
            P(),
        ),
        check_vma=False,
    )
```

profile of v0, /device:TPU:13, one launch (start us, length us, event | category | flops | bytes accessed | tf_op | source)
XLA Modules:
  0.0 1828.6 jit_solution(2981906982083309824)
XLA Ops:
  11.7 31.3 %all-gather = bf16[32,1,256]{2,1,0:T(2,128)(2,1)S(1)} all-gather(bf16[1,1,256]{2,1,0:T(2,128)(2,1)S(1)} %reshape.258), channel_id=1, replica_groups=mesh['dp'=8,'fsdp'=4] {'dp','fsdp'}, dimensions={0}, use_global_device_ids=true | all-gather | bytes 16896 | tf_op jit(solution)/shard_map/all_gather | solution.py:123
  46.0 21.0 %all-gather.5.cloned.1.call-done = bf16[100,8192]{1,0:T(8,128)(2,1)} async-done(((bf16[100,256]{1,0:T(8,128)(2,1)}), bf16[100,8192]{1,0:T(8,128)(2,1)}) %all-gather.5.cloned.1.call-update) | async-done | bytes 1638416 | tf_op jit(solution)/shard_map/all_gather | solution.py:122
  75.8 186.7 %all-gather.7.cloned.1.call-done = bf16[2048,8192]{1,0:T(8,128)(2,1)} async-done(((bf16[64,8192]{1,0:T(8,128)(2,1)}), bf16[2048,8192]{1,0:T(8,128)(2,1)}) %all-gather.7.cloned.1.call-update) | async-done | bytes 33554448 | tf_op jit(solution)/shard_map/all_gather | solution.py:120
  268.4 101.6 %while.84 = (s32[]{:T(128)}, bf16[32,2048]{1,0:T(8,128)(2,1)S(1)}, f32[32,2048]{1,0:T(8,128)S(1)}, f32[6,32,8192]{2,1,0:T(8,128)}, bf16[6,32,2048]{2,1,0:T(8,128...) while((s32[]{:T(128)}, bf16[32,2048]{1,0:T(8,128)(2,1)S(1)}, ...), condition=%wide.region_1.2_spmd.clone, body=%wide.region_0.1_spmd.clone.sunk | while | flops 1075642368 | bytes 40502880 | solution.py:45
  269.3 15.1 bitcast_dynamic-update-slice_fusion.18
  286.2 15.0 bitcast_dynamic-update-slice_fusion.18
  303.1 15.3 bitcast_dynamic-update-slice_fusion.18
  320.2 15.0 bitcast_dynamic-update-slice_fusion.18
  337.1 15.1 bitcast_dynamic-update-slice_fusion.18
  377.1 101.5 %while.85 = (s32[]{:T(128)}, bf16[32,2048]{1,0:T(8,128)(2,1)S(1)}, f32[32,2048]{1,0:T(8,128)S(1)}, f32[6,32,8192]{2,1,0:T(8,128)}, bf16[6,32,2048]{2,1,0:T(8,128...) while((s32[]{:T(128)}, bf16[32,2048]{1,0:T(8,128)(2,1)S(1)}, ...), condition=%wide.region_7.8_spmd.clone, body=%wide.region_6.7_spmd.clone.sunk | while | flops 1075642368 | bytes 40502496 | solution.py:45
  394.8 15.1 bitcast_dynamic-update-slice_fusion.22
  428.7 15.0 bitcast_dynamic-update-slice_fusion.22
  489.6 128.1 %while.86 = (s32[]{:T(128)}, f32[32,2048]{1,0:T(8,128)}, f32[32,2048]{1,0:T(8,128)}, bf16[6,32,8192]{2,1,0:T(8,128)(2,1)}, f32[6,32,2048]{2,1,0:T(8,128)}, /*ind...) while((s32[]{:T(128)}, f32[32,2048]{1,0:T(8,128)}, ...), condition=%wide.region_14.15_spmd.clone, body=%wide.region_13.14_spmd.clone.sunk | while | flops 1080754176 | bytes 41419436 | solution.py:91
  494.2 15.9 convolution_multiply_fusion.4
  515.5 15.9 convolution_multiply_fusion.4
  536.9 15.9 convolution_multiply_fusion.4
  558.3 15.9 convolution_multiply_fusion.4
  579.7 15.9 convolution_multiply_fusion.4
  601.0 15.9 convolution_multiply_fusion.4
  623.2 119.1 %while.87 = (s32[]{:T(128)}, f32[32,2048]{1,0:T(8,128)S(1)}, f32[32,2048]{1,0:T(8,128)S(1)}, bf16[6,32,8192]{2,1,0:T(8,128)(2,1)}, f32[6,32,2048]{2,1,0:T(8,128)...) while((s32[]{:T(128)}, f32[32,2048]{1,0:T(8,128)S(1)}, ...), condition=%wide.region_16.17_spmd.clone, body=%wide.region_15.16_spmd.clone.sunk | while | flops 1080754176 | bytes 41419436 | solution.py:91
  627.0 15.2 convolution_multiply_fusion.5
  646.9 15.2 convolution_multiply_fusion.5
  666.7 15.2 convolution_multiply_fusion.5
  686.6 15.2 convolution_multiply_fusion.5
  706.4 15.2 convolution_multiply_fusion.5
  726.3 15.2 convolution_multiply_fusion.5
  759.3 29.6 %fusion.90 = f32[2048,8192]{1,0:T(8,128)} fusion(bf16[192,8192]{1,0:T(8,128)(2,1)S(1)} %bitcast.233, bf16[192,8192]{1,0:T(8,128)(2,1)} %bitcast.236, bf16[192,2048]{1,0:T(8,128)(2,1)} %bitcast.255, bf16[192,2048]{1,0:T(8,128)(2,1)} %bitcast.256), kind=kOutput, calls=%fused_computation.151 | convolution fusion | flops 12900630528 | bytes 74973184 | tf_op jit(solution)/shard_map/dot_general | solution.py:18
  796.3 40.1 %all-reduce.1 = (f32[]{:T(128)}, f32[8192]{0:T(1024)S(1)}, f32[275]{0:T(512)}) all-reduce(f32[]{:T(128)S(6)} %add.232, f32[8192]{0:T(1024)S(1)} %add.235, f32[275]{0:T(512)S(1)} %add.237), channel_id=1, replica_groups=mesh['dp'=8,'fsdp'=4] {'dp','fsdp'}, use_global_device_ids=true, to_apply=%region_12.13 | all-reduce | flops 8468 | bytes 67744 | tf_op jit(solution)/shard_map/psum | solution.py:155
  840.4 28.1 %all-reduce.4.cloned.1.call-done = f32[275,100]{1,0:T(8,128)} async-done(((f32[275,100]{1,0:T(8,128)}), f32[275,100]{1,0:T(8,128)}) %all-reduce.4.cloned.1.call-update) | async-done | bytes 110016 | tf_op jit(solution)/shard_map/psum | solution.py:155
  868.6 108.1 %reduce-scatter.8.cloned.1.call-done = f32[64,275]{1,0:T(8,128)} async-done(((f32[2048,275]{1,0:T(8,128)}), f32[64,275]{1,0:T(8,128)}) %reduce-scatter.8.cloned.1.call-update) | async-done | bytes 70416 | tf_op jit(solution)/shard_map/reduce_scatter | solution.py:151
  976.7 112.9 %reduce-scatter.4.cloned.1.call-done = f32[100,256]{1,0:T(8,128)} async-done(((f32[100,8192]{1,0:T(8,128)}), f32[100,256]{1,0:T(8,128)}) %reduce-scatter.4.cloned.1.call-update) | async-done | bytes 102416 | tf_op jit(solution)/shard_map/reduce_scatter | solution.py:152
  1089.5 729.5 %reduce-scatter.6.cloned.1.call-done = f32[64,8192]{1,0:T(8,128)} async-done(((f32[2048,8192]{1,0:T(8,128)}), f32[64,8192]{1,0:T(8,128)}) %reduce-scatter.6.cloned.1.call-update) | async-done | bytes 2097168 | tf_op jit(solution)/shard_map/reduce_scatter | solution.py:147
  (257 shorter events, 229.4 us)
Async XLA Ops:
  7.2 37.6 %copy-start = (bf16[275,100]{1,0:T(8,128)(2,1)S(1)}, bf16[275,100]{1,0:T(8,128)(2,1)}, u32[]{:S(2)}) copy-start(bf16[275,100]{1,0:T(8,128)(2,1)} %param.20) | copy-start | bytes 165004
  7.2 59.8 %all-gather.5.cloned.1.call-start = ((), (), s32[]{:S(2)}) async-start(), calls=%async_computation.3 | async-start | bytes 1757184 | tf_op jit(solution)/shard_map/all_gather | solution.py:122
  7.9 254.6 %all-gather.7.cloned.1.call-start = ((), (), s32[]{:S(2)}) async-start(), calls=%async_computation.4 | async-start | bytes 34603008 | tf_op jit(solution)/shard_map/all_gather | solution.py:120
  8.7 470.0 %all-gather.9.cloned.1.call-start = ((), (), s32[]{:S(2)}) async-start(), calls=%async_computation.5 | async-start | bytes 1622016 | tf_op jit(solution)/shard_map/all_gather | solution.py:121
  9.4 859.2 %all-reduce.4.cloned.1.call-start = ((), (), s32[]{:S(2)}) async-start(), calls=%async_computation.6 | async-start | bytes 286720 | tf_op jit(solution)/shard_map/psum | solution.py:155
  11.1 33.7 %copy-start.22 = (s32[192]{0:T(256)}, s32[192]{0:T(256)S(1)}, u32[]{:S(2)}) copy-start(s32[192]{0:T(256)S(1)} %eq.60) | copy-start | bytes 2308
  44.8 27.4 %copy-start.24 = (s32[192]{0:T(256)}, s32[192]{0:T(256)S(1)}, u32[]{:S(2)}) copy-start(s32[192]{0:T(256)S(1)} %eq.68) | copy-start | bytes 2308
  45.0 27.1 %copy-start.14 = (bf16[192,100]{1,0:T(8,128)(2,1)}, bf16[192,100]{1,0:T(8,128)(2,1)S(1)}, u32[]{:S(2)}) copy-start(bf16[192,100]{1,0:T(8,128)(2,1)S(1)} %convolution_convert_fusion.1) | copy-start | bytes 115204
  45.3 26.9 %copy-start.12 = (bf16[192,100]{1,0:T(8,128)(2,1)}, bf16[192,100]{1,0:T(8,128)(2,1)S(1)}, u32[]{:S(2)}) copy-start(bf16[192,100]{1,0:T(8,128)(2,1)S(1)} %convolution_convert_fusion) | copy-start | bytes 115204
  67.0 5.1 copy-start.3
  370.0 3.3 copy-start.11
  370.0 113.2 %copy-start.6 = (bf16[6,32,2048]{2,1,0:T(8,128)(2,1)}, bf16[6,32,2048]{2,1,0:T(8,128)(2,1)S(1)}, u32[]{:S(2)}) copy-start(bf16[6,32,2048]{2,1,0:T(8,128)(2,1)S(1)} %get-tuple-element.526) | copy-start | bytes 2359300
  478.6 0.9 copy-start.7
  479.5 6.2 copy-start.5
  481.8 5.8 copy-start.16
  482.5 5.1 copy-start.19
  489.6 128.1 %copy-start.8 = (bf16[6,32,2048]{2,1,0:T(8,128)(2,1)S(1)}, bf16[6,32,2048]{2,1,0:T(8,128)(2,1)}, u32[]{:S(2)}) copy-start(bf16[6,32,2048]{2,1,0:T(8,128)(2,1)} %copy-done.7) | copy-start | bytes 2359300
  489.6 128.8 %copy-start.18 = (s32[192]{0:T(256)S(1)}, s32[192]{0:T(256)}, u32[]{:S(2)}) copy-start(s32[192]{0:T(256)} %eq.72) | copy-start | bytes 2308
  619.3 3.9 copy-start.9
  619.3 3.9 copy-start.10
  742.3 3.5 copy-start.23
  742.3 4.1 copy-start.2
  742.3 4.1 copy-start.4
  745.9 1.6 copy-start.25
  748.8 227.9 %reduce-scatter.8.cloned.1.call-start = ((), (), s32[]{:S(2)}) async-start(), calls=%async_computation.9 | async-start | bytes 3244032 | tf_op jit(solution)/shard_map/reduce_scatter | solution.py:151
  753.4 0.8 copy-start.15
  753.4 3.3 copy-start.13
  753.4 336.1 %reduce-scatter.4.cloned.1.call-start = ((), (), s32[]{:S(2)}) async-start(), calls=%async_computation.7 | async-start | bytes 3514368 | tf_op jit(solution)/shard_map/reduce_scatter | solution.py:152
  759.2 1059.8 %reduce-scatter.6.cloned.1.call-start = ((), (), s32[]{:S(2)}) async-start(), calls=%async_computation.8 | async-start | bytes 69206016 | tf_op jit(solution)/shard_map/reduce_scatter | solution.py:147
  788.9 0.7 copy-start.20
  793.3 3.0 copy-start.21
  793.4 1027.2 %copy-start.1 = (bf16[275,100]{1,0:T(8,128)(2,1)S(1)}, bf16[275,100]{1,0:T(8,128)(2,1)}, u32[]{:S(2)}) copy-start(bf16[275,100]{1,0:T(8,128)(2,1)} %param.20) | copy-start | bytes 165004
  (1 other events, 0.7 us)
Sparse Core Ops, SparseCore 0:
  10.9 56.0 all-gather.4
  69.9 192.5 all-gather.6
  265.4 54.0 all-gather.8
  748.9 119.6 all-reduce.3
  874.4 102.2 reduce-scatter.7
  979.4 110.0 reduce-scatter.3
  1092.6 726.3 reduce-scatter.5
where the time goes:
time: 1840 us; the launch traced here: 1830 us
  waiting for transfers between devices  1190 us (65%)
  matrix products  431 us (23%)
  other arithmetic  76.5 us (4%)
  blocking collectives  71.4 us (4%)
  local copies, waits for them, and re-layouts  41.2 us (2%)
  between operations  18.9 us (1%)
    reduce_scatter x1, waiting for transfers between devices, per_device(): lax.psum_scatter(dot_left_t(prev_all, pre_all), ('dp', 'fsdp'), scatter_d...  729 us
    dot_general x16, matrix products, dot_right_t(): lax.dot_general(left, right, (((1,), (1,)), ((), ())), preferred_element_...  195 us
    dot_general x18, matrix products, dot_plain(): return jnp.dot(left, right, preferred_element_type=jnp.float32)  193 us
    all_gather x1, waiting for transfers between devices, per_device(): lax.all_gather(w_rec, ('dp', 'fsdp'), axis=0, tiled=True)  187 us
    reduce_scatter x1, waiting for transfers between devices, per_device(): lax.psum_scatter(sums[1], ('dp', 'fsdp'), scatter_dimension=1, tiled=True)  113 us
    reduce_scatter x1, waiting for transfers between devices, per_device(): lax.psum_scatter(sums[0], ('dp', 'fsdp'), scatter_dimension=0, tiled=True)  108 us
    dot_general x5, matrix products, dot_left_t(): lax.dot_general(left, right, (((0,), (0,)), ((), ())), preferred_element_...  41.6 us
    psum x1, blocking collectives, per_device(): lax.psum((sums[3], sums[4], sums[5]), ('dp', 'fsdp'))  40.1 us
  transfers between devices with their start and end apart: 7, of which 6 were waited for; matrix products, arithmetic and copies ran while one was open for 15% of the time, Pallas kernels for 0%

commit v1 on v0

--- a/solution.py
+++ b/solution.py
@@ -1,7 +1,840 @@
+import functools
+
 import jax
 import jax.numpy as jnp
 from jax import lax
+from jax.experimental import pallas as pl
+from jax.experimental.pallas import tpu as pltpu
 from jax.sharding import PartitionSpec as P
+
+MESH = pl.DeviceIdType.MESH
+NN = ((1,), (0,))
+NT = ((1,), (1,))
+TN = ((0,), (0,))
+F32 = jnp.float32
+BF = jnp.bfloat16
+
+VPAD = 384
+EPAD = 128
+RING = 4
+SMALL = 112
+
+
+def mm(left, right, dims):
+    return lax.dot_general(left, right, (dims, ((), ())), preferred_element_type=F32)
+
+
+def sigmoid(v):
+    return 0.5 * jnp.tanh(0.5 * v) + 0.5
+
+
+def lstm_kernel(
+    steps, rows,
+    w_rec, w_in, w_dec, emb_t, bias_dec, ids_in,
+    out_rec, out_in, out_dec, out_hid, out_small,
+    W, WIN, WDEC, IDS, H, HT, HTS, HSEND, A, C, D, DS, DRAW, DL,
+    PR, STG, OWN, DCN, SY, RY, SM, RM, EMBT, LV, BD, GWD, GS, GY, GM, DWI, IS, IY, IM, RSM,
+    s_ids, r_ids, s_win, r_win, s_wa, r_wa, s_wm, r_wm, s_wy, r_wy, s_ws, r_ws,
+    s_da, r_da, s_dm, r_dm, s_dy, r_dy, s_ds, r_ds, s_h, r_h, s_ht, r_ht, s_d, r_d,
+    s_pr, r_pr, s_gd, r_gd, s_gi, r_gi, s_sm, r_sm, s_ry, r_ry, s_rm, r_rm, s_ra, r_ra,
+    l_sem, hid_sem,
+):
+    last = steps - 1
+    dp, fs = lax.axis_index("dp"), lax.axis_index("fsdp")
+    z, x, y, c = dp // 2, dp % 2, fs // 2, fs % 2
+    zh = z // 2
+    a = z + zh * (3 - 2 * z)
+
+    def dev(zz, xx, yy, cc):
+        return (zz * 2 + xx, yy * 2 + cc)
+
+    def block(zz, xx, yy, cc):
+        return zz * 8 + xx * 4 + yy * 2 + cc
+
+    def kx(k):
+        return x + (k % 2) * (1 - 2 * x)
+
+    def kz(k):
+        return z + (k // 2) * (1 - 2 * (z % 2))
+
+    def ka(k):
+        return a + (k // 2) * (1 - 2 * a)
+
+    def kdev(k):
+        return dev(kz(k), kx(k), y, c)
+
+    def member(k):
+        return 2 * kx(k) + ka(k)
+
+    def unit_block(k, j):
+        return 2 * (ka(k) + j * (3 - 2 * ka(k))) + kx(k)
+
+    def lanes(ub):
+        return pl.ds(pl.multiple_of(256 * ub, 256), 256)
+
+    mir, ydev, sib = dev(3 - z, x, y, c), dev(z, x, 1 - y, c), dev(z, x, y, 1 - c)
+    perm = dev(2 * x + y, c, z // 2, z % 2)
+    back = dev(2 * y + c, z // 2, z % 2, x)
+    stays = jnp.logical_and(perm[0] == dp, perm[1] == fs)
+    moved = jnp.logical_not(stays)
+
+    def rc(src, dst, ss, rs, to):
+        return pltpu.make_async_remote_copy(
+            src_ref=src, dst_ref=dst, send_sem=ss, recv_sem=rs, device_id=to, device_id_type=MESH
+        )
+
+    barrier = pltpu.get_barrier_semaphore()
+
+    def greet(to):
+        pl.semaphore_signal(barrier, inc=1, device_id=to, device_id_type=MESH)
+
+    for k in (1, 2, 3):
+        greet(kdev(k))
+    for to in (mir, ydev, sib):
+        greet(to)
+
+    @pl.when(moved)
+    def _():
+        greet(perm)
+        greet(back)
+
+    pl.semaphore_wait(barrier, 6 + 2 * moved.astype(jnp.int32))
+
+    me = block(z, x, y, c)
+
+    def w_slot(b):
+        return W.at[:, pl.ds(pl.multiple_of(64 * b, 64), 64), :]
+
+    def d_slot(b):
+        return WDEC.at[pl.ds(pl.multiple_of(64 * b, 64), 64), :]
+
+    def wa(k, j, b):
+        return rc(
+            w_rec.at[unit_block(k, j)],
+            W.at[pl.ds(4 * j, 4), pl.ds(pl.multiple_of(64 * b, 64), 64), :],
+            s_wa.at[k - 1, j], r_wa.at[k - 1, j], kdev(k),
+        )
+
+    def ids_copy(k, mem):
+        return rc(ids_in, IDS.at[:, mem], s_ids.at[k - 1], r_ids.at[k - 1], kdev(k))
+
+    def own_w(j):
+        return pltpu.make_async_copy(
+            w_rec.at[unit_block(0, j)],
+            W.at[pl.ds(4 * j, 4), pl.ds(pl.multiple_of(64 * me, 64), 64), :],
+            l_sem.at[j],
+        )
+
+    own_w(0).start()
+    own_w(1).start()
+    for k in (1, 2, 3):
+        ids_copy(k, member(0)).start()
+
+    def win_perm(jj, gy, gc):
+        return rc(w_in, WIN.at[jj, gy, gc], s_win.at[0], r_win.at[0], perm)
+
+    def win_local():
+        return pltpu.make_async_copy(w_in, WIN.at[x, z // 2, z % 2], l_sem.at[2])
+
+    @pl.when(moved)
+    def _():
+        win_perm(x, z // 2, z % 2).start()
+
+    @pl.when(stays)
+    def _():
+        win_local().start()
+
+    for k in (3, 1, 2):
+        for j in (0, 1):
+            wa(k, j, me).start()
+
+    def to_mir(k):
+        b = block(kz(k), kx(k), y, c)
+        return rc(w_slot(b), w_slot(b), s_wm.at[k], r_wm.at[k], mir)
+
+    def from_mir(k):
+        b = block(3 - kz(k), kx(k), y, c)
+        return rc(w_slot(b), w_slot(b), s_wm.at[k], r_wm.at[k], mir)
+
+    def group_block(i, yy, cc):
+        k, far = i % 4, i // 4
+        zz = kz(k)
+        return block(zz + far * (3 - 2 * zz), kx(k), yy, cc)
+
+    def to_y(i, slot=None):
+        b = group_block(i, y, c)
+        return rc(w_slot(b), w_slot(b), s_wy.at[i], r_wy.at[i], ydev)
+
+    def from_y(i):
+        b = group_block(i, 1 - y, c)
+        return rc(w_slot(b), w_slot(b), s_wy.at[i], r_wy.at[i], ydev)
+
+    def to_s(i):
+        b = group_block(i % 8, y + (i // 8) * (1 - 2 * y), c)
+        return rc(w_slot(b), w_slot(b), s_ws.at[i], r_ws.at[i], sib)
+
+    def from_s(i):
+        b = group_block(i % 8, y + (i // 8) * (1 - 2 * y), 1 - c)
+        return rc(w_slot(b), w_slot(b), s_ws.at[i], r_ws.at[i], sib)
+
+    own_w(0).wait()
+    own_w(1).wait()
+    to_mir(0).start()
+    to_y(0).start()
+    to_s(0).start()
+
+    IDS[:, member(0)] = ids_in[...]
+
+    for k in (1, 2, 3):
+        for j in (0, 1):
+            wa(k, j, block(kz(k), kx(k), y, c)).wait_recv()
+        to_mir(k).start()
+        to_y(k).start()
+        to_s(k).start()
+
+    def da(k, b):
+        return rc(w_dec, d_slot(b), s_da.at[k - 1], r_da.at[k - 1], kdev(k))
+
+    for k in (1, 2, 3):
+        da(k, me).start()
+    own_dec = pltpu.make_async_copy(w_dec, d_slot(me), l_sem.at[3])
+    own_dec.start()
+
+    def win_mir(jj):
+        return rc(WIN.at[jj, y, c], WIN.at[jj, y, c], s_win.at[1], r_win.at[1], mir)
+
+    def win_y(yy):
+        return rc(WIN.at[:, yy, c], WIN.at[:, yy, c], s_win.at[2], r_win.at[2], ydev)
+
+    def win_s(cc):
+        return rc(WIN.at[:, :, cc], WIN.at[:, :, cc], s_win.at[3], r_win.at[3], sib)
+
+    @pl.when(moved)
+    def _():
+        win_perm(zh, y, c).wait_recv()
+
+    @pl.when(stays)
+    def _():
+        win_local().wait()
+
+    win_mir(zh).start()
+
+    for k in (1, 2, 3):
+        ids_copy(k, member(k)).wait_recv()
+    lane = lax.broadcasted_iota(jnp.int32, (rows, 128), 1)
+    wide = lax.broadcasted_iota(jnp.int32, (rows, VPAD), 1).astype(F32)
+
+    def column(at, s):
+        packed = IDS[s].reshape(rows, 128)
+        return jnp.sum(jnp.where(lane == at, packed, 0).astype(F32), axis=1, keepdims=True)
+
+    def keep_of(t, s):
+        return 1.0 - column(8 + t, s)
+
+    def letter(t, s):
+        return jnp.where(column(t, s) == wide, 1.0, 0.0).astype(BF)
+
+    EMBT[...] = jnp.zeros_like(EMBT)
+    LV[...] = jnp.zeros_like(LV)
+    BD[...] = jnp.zeros_like(BD)
+    GWD[...] = jnp.zeros_like(GWD)
+    DWI[...] = jnp.zeros_like(DWI)
+    DCN[...] = jnp.zeros_like(DCN)
+
+    win_mir(1 - zh).wait_recv()
+    win_y(y).start()
+    from_y(0).wait_recv()
+    to_s(8).start()
+    from_mir(0).wait_recv()
+    to_y(4).start()
+    to_s(4).start()
+    from_y(1).wait_recv()
+    to_s(9).start()
+    win_y(1 - y).wait_recv()
+    win_s(c).start()
+    win_s(1 - c).wait_recv()
+
+    def h_copy(t, s, k, j, ub):
+        part = H.at[t % RING, s, :, lanes(ub)]
+        return rc(part, part, s_h.at[t, s, k - 1, j], r_h.at[t, s, k - 1, j], kdev(k))
+
+    def wait_h(t, s):
+        for k in (1, 2, 3):
+            for j in (0, 1):
+                h_copy(t, s, k, j, unit_block(k, j)).wait_recv()
+
+    def gates(t, s, first):
+        keep = None if first else keep_of(t, s)
+        feature = mm(letter(t, s), emb_t[...], NT).astype(BF)
+        for j in (0, 1):
+            pre = []
+            for g in range(4):
+                drive = mm(feature, WIN[j, g // 2, g % 2], NN)
+                if not first:
+                    drive = drive + keep * mm(H[(t - 1) % RING, s], W[4 * j + g], NN)
+                pre.append(drive)
+            s_i, s_f, t_g, s_o = sigmoid(pre[0]), sigmoid(pre[1]), jnp.tanh(pre[2]), sigmoid(pre[3])
+            cell = s_i * t_g
+            if not first:
+                cell = s_f * (C[t - 1, s, j] * keep) + cell
+            for g, v in enumerate((s_i, s_f, t_g, s_o)):
+                A[t, s, 4 * j + g] = v
+            C[t, s, j] = cell
+            ub = unit_block(0, j)
+            H[t % RING, s, :, lanes(ub)] = (s_o * jnp.tanh(cell)).astype(BF)
+            for k in (3, 1, 2):
+                h_copy(t, s, k, j, ub).start()
+
+    gates(0, 0, True)
+    gates(0, 1, True)
+
+    from_y(2).wait_recv()
+    to_s(10).start()
+    from_mir(1).wait_recv()
+    to_y(5).start()
+    to_s(5).start()
+    from_y(3).wait_recv()
+    to_s(11).start()
+    from_mir(2).wait_recv()
+    to_y(6).start()
+    to_s(6).start()
+    from_y(4).wait_recv()
+    to_s(12).start()
+    from_mir(3).wait_recv()
+    to_y(7).start()
+    to_s(7).start()
+
+    def dec_mir(k, far):
+        zz = kz(k)
+        b = block(zz + far * (3 - 2 * zz), kx(k), y, c)
+        return rc(d_slot(b), d_slot(b), s_dm.at[k], r_dm.at[k], mir)
+
+    def dec_y(i, yy):
+        b = group_block(i, yy, c)
+        return rc(d_slot(b), d_slot(b), s_dy.at[i], r_dy.at[i], ydev)
+
+    def dec_s(i, cc):
+        b = group_block(i % 8, y + (i // 8) * (1 - 2 * y), cc)
+        return rc(d_slot(b), d_slot(b), s_ds.at[i], r_ds.at[i], sib)
+
+    own_dec.wait()
+    dec_mir(0, 0).start()
+    dec_y(0, y).start()
+    dec_s(0, c).start()
+    for k in (1, 2, 3):
+        da(k, block(kz(k), kx(k), y, c)).wait_recv()
+        dec_mir(k, 0).start()
+        dec_y(k, y).start()
+        dec_s(k, c).start()
+
+    for i in (5, 6, 7):
+        from_y(i).wait_recv()
+        to_s(8 + i).start()
+
+    @pl.loop(0, 16)
+    def _(i):
+        from_s(i).wait_recv()
+
+    def released(t, s):
+        hid_copy(t, s).wait()
+        for k in (1, 2, 3):
+            for j in (0, 1):
+                h_copy(t, s, k, j, unit_block(0, j)).wait_send()
+
+    def forward(t, s):
+        wait_h(t - 1, s)
+
+        @pl.when(t >= RING - 1)
+        def _():
+            released(t - (RING - 1), s)
+
+        gates(t, s, False)
+
+    for s in range(2):
+        wait_h(0, s)
+        gates(1, s, False)
+
+    for k in range(4):
+        dec_mir(k, 1).wait_recv()
+        dec_y(4 + k, y).start()
+        dec_s(4 + k, c).start()
+
+    row = lax.broadcasted_iota(jnp.int32, (128, 256), 0)
+    col = lax.broadcasted_iota(jnp.int32, (128, 256), 1)
+
+    def select(cc):
+        yy = y + (row // 64) * (1 - 2 * y)
+        return jnp.where(col == 64 * (2 * yy + cc) + row % 64, 1.0, 0.0).astype(BF)
+
+    def lane_slot(t, s):
+        return pl.ds(pl.multiple_of((2 * t + s) * rows, rows), rows)
+
+    def ht_copy(t, s, slot):
+        return rc(HSEND.at[slot], HTS.at[:, :, lane_slot(t, s)], s_ht.at[t, s], r_ht.at[t, s], sib)
+
+    def hid_copy(t, s):
+        mine = H.at[t % RING, s, pl.ds(pl.multiple_of(32 * member(0), 32), 32), :]
+        return pltpu.make_async_copy(mine, out_hid.at[s, t], hid_sem.at[t, s])
+
+    def logits_of(t, s):
+        scores = mm(H[t % RING, s], WDEC[...], NN) + bias_dec[0:1, :]
+        top = jnp.max(scores, axis=1, keepdims=True)
+        shifted = jnp.exp(scores - top)
+        summed = jnp.sum(shifted, axis=1, keepdims=True)
+        goal = jnp.where(column(16 + t, s) == wide, 1.0, 0.0)
+        picked = jnp.sum(goal * scores, axis=1, keepdims=True)
+        LV[...] += jnp.broadcast_to(top + jnp.log(summed) - picked, (rows, 128))
+        DL[t, s] = (shifted / summed - goal).astype(BF)
+
+    def decoder_side(t, s):
+        hid_copy(t, s).start()
+        grad = DL[t, s]
+        BD[...] += mm(jnp.ones((8, rows), BF), grad, NN)
+        for j in (0, 1):
+            GWD[j] += mm(H[t % RING, s, :, lanes(unit_block(0, j))], grad, TN).reshape(2, 2, 64, VPAD)
+
+    def transposed_side(t, s):
+        slot = s
+        mine, other = select(c), select(1 - c)
+
+        @pl.when(t >= 1)
+        def _():
+            ht_copy(t - 1, s, slot).wait_send()
+
+        for tile in range(8):
+            part = H[t % RING, s, :, 256 * tile : 256 * (tile + 1)]
+            HT[tile, :, lane_slot(t, s)] = mm(mine, part, NT).astype(BF)
+            HSEND[slot, tile] = mm(other, part, NT).astype(BF)
+        ht_copy(t, s, slot).start()
+
+    for i in range(8):
+        dec_y(i, 1 - y).wait_recv()
+        dec_s(8 + i, c).start()
+
+    @pl.loop(0, 16)
+    def _(i):
+        dec_s(i, 1 - c).wait_recv()
+
+    @pl.loop(4, 2 * steps)
+    def _(i):
+        t, s = i // 2, i % 2
+        forward(t, s)
+        logits_of(t - 2, s)
+        decoder_side(t - 2, s)
+        transposed_side(t - 2, s)
+
+    @pl.loop(0, 2)
+    def _(s):
+        logits_of(last - 1, s)
+        decoder_side(last - 1, s)
+        transposed_side(last - 1, s)
+
+    def pr_copy(t, s, k, j):
+        return rc(STG.at[s, k - 1, j], PR.at[t % 2, s, k - 1, j], s_pr.at[t, s, k - 1, j], r_pr.at[t, s, k - 1, j], kdev(k))
+
+    def d_copy(t, s):
+        return rc(D.at[:, t - 1, s], DS.at[:, t - 1, s], s_d.at[t, s], r_d.at[t, s], sib)
+
+    def backward(t, s, newest, oldest):
+        if not newest:
+            for k in (1, 2, 3):
+                for j in (0, 1):
+                    pr_copy(t + 1, s, k, j).wait_recv()
+        keep = keep_of(t, s)
+        for j in (0, 1):
+            up = WDEC[lanes(unit_block(0, j)), :]
+            dh = mm(DL[t, s], up, NT)
+            if not newest:
+                rest = PR[(t + 1) % 2, s, 0, j].astype(F32) + PR[(t + 1) % 2, s, 1, j].astype(F32)
+                rest = rest + PR[(t + 1) % 2, s, 2, j].astype(F32)
+                dh = dh + (OWN[s, j] + rest)
+            s_i, s_f, t_g, s_o = (A[t, s, 4 * j + g] for g in range(4))
+            t_c = jnp.tanh(C[t, s, j])
+            d_o = dh * t_c
+            d_c = dh * s_o * (1.0 - t_c * t_c)
+            if not newest:
+                d_c = d_c + DCN[s, j]
+            d_i = d_c * t_g * s_i * (1.0 - s_i)
+            d_g = d_c * s_i * (1.0 - t_g * t_g)
+            d_o = d_o * s_o * (1.0 - s_o)
+            if oldest:
+                d_f = jnp.zeros_like(d_i)
+            else:
+                d_f = d_c * (C[t - 1, s, j] * keep) * s_f * (1.0 - s_f)
+                DCN[s, j] = keep * (d_c * s_f)
+            for g, v in enumerate((d_i, d_f, d_g, d_o)):
+                low = v.astype(BF)
+                DRAW[4 * j + g] = low
+                if not oldest:
+                    D[4 * j + g, t - 1, s] = low * keep.astype(BF)
+        if oldest:
+            return
+        d_copy(t, s).start()
+        if not newest:
+            for k in (1, 2, 3):
+                for j in (0, 1):
+                    pr_copy(t + 1, s, k, j).wait_send()
+        for k in (3, 1, 2, 0):
+            for j in (0, 1):
+                ub = unit_block(k, j)
+                total = None
+                for q in range(8):
+                    term = mm(D[q, t - 1, s], W[q, lanes(ub), :], NT)
+                    total = term if total is None else total + term
+                if k == 0:
+                    OWN[s, j] = total
+                else:
+                    STG[s, k - 1, j] = total.astype(BF)
+                    pr_copy(t, s, k, j).start()
+
+    def input_side(t, s):
+        onehot = letter(t, s)
+        feat_t = mm(emb_t[...], onehot, NT).astype(BF)
+        grad_t = None
+        for q in range(8):
+            jj, gy, gc = q // 4, (q // 2) % 2, q % 2
+            DWI[jj, gy, gc] += mm(feat_t, DRAW[q], NN)
+            term = mm(WIN[jj, gy, gc], DRAW[q], NT)
+            grad_t = term if grad_t is None else grad_t + term
+        high = grad_t.astype(BF)
+        low = (grad_t - high.astype(F32)).astype(BF)
+        EMBT[...] += mm(high, onehot, NN) + mm(low, onehot, NN)
+
+    for s in range(2):
+        wait_h(last, s)
+        logits_of(last, s)
+        backward(last, s, True, False)
+        input_side(last, s)
+    for s in range(2):
+        decoder_side(last, s)
+
+    def gd_s():
+        return rc(GWD.at[:, :, 1 - c], GS, s_gd.at[0], r_gd.at[0], sib)
+
+    def gd_y():
+        return rc(GWD.at[:, 1 - y, c], GY, s_gd.at[1], r_gd.at[1], ydev)
+
+    def gd_m():
+        return rc(GWD.at[1 - zh, y, c], GM, s_gd.at[2], r_gd.at[2], mir)
+
+    gd_s().start()
+
+    @pl.loop(0, 2 * (steps - 2))
+    def _(i):
+        t, s = last - 1 - i // 2, i % 2
+        backward(t, s, False, False)
+        input_side(t, s)
+
+        @pl.when(i == 1)
+        def _():
+            gd_s().wait_recv()
+            GWD[:, :, c] += GS[...]
+            gd_y().start()
+
+        @pl.when(i == 3)
+        def _():
+            gd_y().wait_recv()
+            GWD[:, y, c] += GY[...]
+            gd_m().start()
+
+        @pl.when(i == 5)
+        def _():
+            gd_m().wait_recv()
+            out_dec[...] = GWD[zh, y, c] + GM[...]
+
+    @pl.loop(0, 2 * (steps - 1))
+    def _(i):
+        ht_copy(i // 2, i % 2, 0).wait_recv()
+        d_copy(1 + i // 2, i % 2).wait_recv()
+
+    depth = 2 * (steps - 1) * rows
+
+    def kept(q):
+        return A.at[2 + q // 4, (q % 4) // 2, :, pl.ds(pl.multiple_of(64 * (q % 2), 64), 64), :]
+
+    def tile_of(q):
+        k, near = q % 4, q // 4
+        zz = kz(k)
+        return 2 * (3 - zz + near * (2 * zz - 3)) + kx(k)
+
+    def ry_copy(q):
+        return rc(SY.at[q % 4], RY.at[q], s_ry.at[q], r_ry.at[q], ydev)
+
+    def rm_copy(k):
+        return rc(SM.at[k], RM.at[k], s_rm.at[k], r_rm.at[k], mir)
+
+    def ra_copy(k, j, src_kind):
+        src = A.at[3, k // 2, pl.ds(4 * j, 4), pl.ds(pl.multiple_of(64 * (k % 2), 64), 64), :]
+        return rc(src, out_rec.at[unit_block(src_kind, j)], s_ra.at[k - 1, j], r_ra.at[k - 1, j], kdev(k))
+
+    def ra_own(j):
+        src = A.at[3, 0, pl.ds(4 * j, 4), pl.ds(0, 64), :]
+        return pltpu.make_async_copy(src, out_rec.at[unit_block(0, j)], l_sem.at[4 + j])
+
+    def make_tile(q):
+        tile = tile_of(q)
+        left, right = HT[tile], HTS[tile]
+        hold = kept(q)
+        if isinstance(q, int):
+            ry_copy(q - 4).wait_send()
+        for n in range(8):
+            grad = mm(left, D[n].reshape(depth, 256), NN) + mm(right, DS[n].reshape(depth, 256), NN)
+            hold[n] = grad[:64]
+            SY[q % 4, n] = grad[64:].astype(BF)
+        ry_copy(q).start()
+
+    def add_y(q):
+        ry_copy(q).wait_recv()
+        hold = kept(q)
+        hold[...] = hold[...] + RY[q].astype(F32)
+
+    @pl.loop(0, 4)
+    def _(i):
+        make_tile(3 - i)
+
+    def pass_on(k):
+        add_y(k)
+        SM[k] = kept(k)[...].astype(BF)
+        rm_copy(k).start()
+
+    for s in range(2):
+        backward(0, s, False, True)
+        input_side(0, s)
+
+    leader = jnp.logical_and(x == 0, a == 0)
+    high_row = lax.broadcasted_iota(jnp.int32, (8, VPAD), 0)
+    loss = jnp.sum(LV[...], axis=0, keepdims=True)
+    loss = jnp.concatenate([loss] * (VPAD // 128), axis=1)
+    extra = jnp.where(high_row == 0, BD[...], jnp.where(high_row == 1, loss, 0.0))
+    out_small[0 : SMALL - 8] = EMBT[0 : SMALL - 8]
+    out_small[SMALL - 8 : SMALL] = jnp.where(leader, extra, 0.0)
+
+    small_to = (sib, ydev, mir, kdev(1), kdev(2))
+
+    def sm_copy(n):
+        return rc(out_small, RSM.at[n], s_sm.at[n], r_sm.at[n], small_to[n])
+
+    def sm_next(n):
+        sm_copy(n).wait()
+        out_small[...] = out_small[...] + RSM[n]
+        if n < 4:
+            sm_copy(n + 1).start()
+
+    sm_copy(0).start()
+
+    live = pl.ds(0, 104)
+
+    def gi_s():
+        return rc(DWI.at[:, :, 1 - c, live], IS, s_gi.at[0], r_gi.at[0], sib)
+
+    def gi_y():
+        return rc(DWI.at[:, 1 - y, c, live], IY, s_gi.at[1], r_gi.at[1], ydev)
+
+    def gi_m():
+        return rc(DWI.at[1 - zh, y, c, live], IM, s_gi.at[2], r_gi.at[2], mir)
+
+    def gi_p():
+        return rc(DWI.at[zh, y, c, live], out_in, s_gi.at[3], r_gi.at[3], back)
+
+    gi_s().start()
+    pass_on(3)
+    gi_s().wait_recv()
+    DWI[:, :, c, 0:104] = DWI[:, :, c, 0:104] + IS[...]
+    gi_y().start()
+    sm_next(0)
+    make_tile(7)
+    pass_on(2)
+    make_tile(6)
+    pass_on(1)
+    make_tile(5)
+    pass_on(0)
+    make_tile(4)
+    gi_y().wait_recv()
+    DWI[:, y, c, 0:104] = DWI[:, y, c, 0:104] + IY[...]
+    gi_m().start()
+    sm_next(1)
+
+    def finish(k):
+        add_y(4 + k)
+        rm_copy(k).wait_recv()
+        hold = kept(4 + k)
+        hold[...] = hold[...] + RM[k].astype(F32)
+        for j in (0, 1):
+            if k == 0:
+                ra_own(j).start()
+            else:
+                ra_copy(k, j, 0).start()
+
+    finish(3)
+    sm_next(2)
+    gi_m().wait_recv()
+    DWI[zh, y, c, 0:104] = DWI[zh, y, c, 0:104] + IM[...]
+
+    @pl.when(moved)
+    def _():
+        gi_p().start()
+
+    @pl.when(stays)
+    def _():
+        out_in[...] = DWI[zh, y, c, 0:104]
+
+    finish(2)
+    sm_next(3)
+    finish(1)
+    sm_next(4)
+    finish(0)
+
+    for k in (1, 2, 3):
+        for j in (0, 1):
+            ra_copy(k, j, k).wait_recv()
+            ra_copy(k, j, 0).wait_send()
+            wa(k, j, me).wait_send()
+            for s in range(2):
+                pr_copy(1, s, k, j).wait_send()
+        ids_copy(k, member(0)).wait_send()
+        da(k, me).wait_send()
+    ra_own(0).wait()
+    ra_own(1).wait()
+
+    @pl.when(moved)
+    def _():
+        gi_p().wait()
+        win_perm(x, z // 2, z % 2).wait_send()
+
+    win_mir(zh).wait_send()
+    win_y(y).wait_send()
+    win_s(c).wait_send()
+    for copy in (gd_s, gd_y, gd_m, gi_s, gi_y, gi_m):
+        copy().wait_send()
+    for s in range(2):
+        ht_copy(last - 1, s, s).wait_send()
+
+    @pl.loop(0, 4)
+    def _(k):
+        to_mir(k).wait_send()
+        dec_mir(k, 0).wait_send()
+        rm_copy(k).wait_send()
+
+    @pl.loop(0, 8)
+    def _(i):
+        to_y(i).wait_send()
+        dec_y(i, y).wait_send()
+
+    @pl.loop(4, 8)
+    def _(q):
+        ry_copy(q).wait_send()
+
+    @pl.loop(0, 16)
+    def _(i):
+        to_s(i).wait_send()
+        dec_s(i, c).wait_send()
+
+    @pl.loop(2 * (steps - RING + 1), 2 * steps)
+    def _(i):
+        released(i // 2, i % 2)
+
+    @pl.loop(0, 2 * (steps - 1))
+    def _(i):
+        d_copy(1 + i // 2, i % 2).wait_send()
+
+
+def fused(chars, resets, targets, embed, w_in, bias_in, w_rec, w_dec, bias_dec):
+    micro, count, steps = chars.shape
+    own_rows, gate_cols = w_rec.shape
+    vocab, emb = embed.shape
+    width = gate_cols // 4
+    members = 4
+    rows = count * members
+    w_rec4 = w_rec.reshape(own_rows, 4, 8, 256).transpose(2, 1, 0, 3)
+    w_in_e = jnp.zeros((EPAD, 256), BF).at[:emb].set(w_in).at[emb].set(bias_in)
+    w_dec_e = jnp.pad(w_dec, ((0, 0), (0, VPAD - vocab)))
+    emb_t = jnp.zeros((EPAD, VPAD), BF).at[:emb, :vocab].set(embed.T).at[emb, :].set(1.0)
+    bias_e = jnp.full((8, VPAD), -1e30, F32).at[:, :vocab].set(bias_dec.astype(F32)[None, :])
+
+    def six(v):
+        return jnp.pad(v, ((0, 0), (0, 0), (0, 8 - steps)))
+
+    ids = jnp.concatenate([six(chars), six(resets), six(targets)], axis=2)
+    ids = jnp.pad(ids, ((0, 0), (0, 0), (0, 128 - 24)))
+
+    vm = pl.BlockSpec(memory_space=pltpu.VMEM)
+    hbm = pl.BlockSpec(memory_space=pl.ANY)
+    dma = pltpu.SemaphoreType.DMA
+    n = steps - 1
+    scratch = [
+        pltpu.VMEM((8, width, 256), BF),
+        pltpu.VMEM((2, 2, 2, EPAD, 256), BF),
+        pltpu.VMEM((width, VPAD), BF),
+        pltpu.VMEM((micro, members, count, 128), jnp.int32),
+        pltpu.VMEM((RING, micro, rows, width), BF),
+        pltpu.VMEM((8, 128, 2 * n * rows), BF),
+        pltpu.VMEM((8, 128, 2 * n * rows), BF),
+        pltpu.VMEM((2, 8, 128, rows), BF),
+        pltpu.VMEM((steps, micro, 8, rows, 256), F32),
+        pltpu.VMEM((steps, micro, 2, rows, 256), F32),
+        pltpu.VMEM((8, n, micro, rows, 256), BF),
+        pltpu.VMEM((8, n, micro, rows, 256), BF),
+        pltpu.VMEM((8, rows, 256), BF),
+        pltpu.VMEM((steps, micro, rows, VPAD), BF),
+        pltpu.VMEM((2, micro, 3, 2, rows, 256), BF),
+        pltpu.VMEM((micro, 3, 2, rows, 256), BF),
+        pltpu.VMEM((micro, 2, rows, 256), F32),
+        pltpu.VMEM((micro, 2, rows, 256), F32),
+        pltpu.VMEM((4, 8, 64, 256), BF),
+        pltpu.VMEM((8, 8, 64, 256), BF),
+        pltpu.VMEM((4, 8, 64, 256), BF),
+        pltpu.VMEM((4, 8, 64, 256), BF),
+        pltpu.VMEM((EPAD, VPAD), F32),
+        pltpu.VMEM((rows, 128), F32),
+        pltpu.VMEM((8, VPAD), F32),
+        pltpu.VMEM((2, 2, 2, 64, VPAD), F32),
+        pltpu.VMEM((2, 2, 64, VPAD), F32),
+        pltpu.VMEM((2, 64, VPAD), F32),
+        pltpu.VMEM((64, VPAD), F32),
+        pltpu.VMEM((2, 2, 2, EPAD, 256), F32),
+        pltpu.VMEM((2, 2, 104, 256), F32),
+        pltpu.VMEM((2, 104, 256), F32),
+        pltpu.VMEM((104, 256), F32),
+        pltpu.VMEM((5, SMALL, VPAD), F32),
+    ]
+    shapes = [
+        (3,), (4,), (3, 2), (4,), (8,), (16,), (3,), (4,), (8,), (16,),
+        (steps, 2, 3, 2), (n, 2), (steps, 2), (steps, 2, 3, 2), (3,), (4,), (5,), (8,), (4,), (3, 2),
+    ]
+    for shape in shapes:
+        scratch += [dma(shape), dma(shape)]
+    scratch += [dma((6,)), dma((steps, 2))]
+    out_rec, out_in, out_dec, out_hid, out_small = pl.pallas_call(
+        functools.partial(lstm_kernel, steps, rows),
+        out_shape=(
+            jax.ShapeDtypeStruct((8, 4, own_rows, 256), F32),
+            jax.ShapeDtypeStruct((104, 256), F32),
+            jax.ShapeDtypeStruct((own_rows, VPAD), F32),
+            jax.ShapeDtypeStruct((micro, steps, count, width), BF),
+            jax.ShapeDtypeStruct((SMALL, VPAD), F32),
+        ),
+        in_specs=[hbm, vm, vm, vm, vm, vm],
+        out_specs=(hbm, vm, vm, hbm, vm),
+        scratch_shapes=scratch,
+        compiler_params=pltpu.CompilerParams(
+            collective_id=0, has_side_effects=True, vmem_limit_bytes=66 * 1000 * 1000
+        ),
+    )(w_rec4, w_in_e, w_dec_e, emb_t, bias_e, ids)
+    everyone = lax.axis_size(("dp", "fsdp"))
+    loss = out_small[SMALL - 7, 0] / (micro * count * steps * everyone)
+    hidden = out_hid.transpose(0, 2, 1, 3)
+    grad_embed = out_small[:emb, :vocab].T
+    grad_rec = out_rec.transpose(2, 1, 0, 3).reshape(own_rows, gate_cols)
+    return (
+        loss,
+        hidden,
+        grad_embed,
+        out_in[:emb],
+        out_in[emb],
+        grad_rec,
+        out_dec[:, :vocab],
+        out_small[SMALL - 8, :vocab],
+    )
 
 
 def dot_plain(left, right):
@@ -108,7 +941,7 @@
     return (grad_dec, grad_in, grad_bias, grad_table, grad_bias_out, flat_prev, flat_pre)
 
 
-def per_device(chars, resets, targets, embed, w_in, bias_in, w_rec, w_dec, bias_dec):
+def general(chars, resets, targets, embed, w_in, bias_in, w_rec, w_dec, bias_dec):
     micro, count, steps = chars.shape
     everyone = lax.axis_size(("dp", "fsdp"))
     sums = None
@@ -168,6 +1001,7 @@
 
 
 def solution(mesh):
+    per_device = fused if (mesh.shape["dp"], mesh.shape["fsdp"]) == (8, 4) else general
     return jax.shard_map(
         per_device,
         mesh=mesh,

time: 1840 us -> 327 us (0.18)
  waiting for transfers between devices: 1190 us -> 0 us
  matrix products: 431 us -> 0 us
  Pallas kernels: 0 us -> 301 us
  other arithmetic: 76.5 us -> 1.37 us
  blocking collectives: 71.4 us -> 0 us
  local copies, waits for them, and re-layouts: 41.2 us -> 18.8 us
    reduce_scatter x3 -> x0, waiting for transfers between devices: 950 us -> none  [the longest x1 729 us: per_device(): lax.psum_scatter(dot_left_t(prev_all, pre_all), ('dp', 'fsdp'), scatter_d...]
    dot_general x41 -> x0, matrix products: 431 us -> none  [the longest x16 195 us: dot_right_t(): lax.dot_general(left, right, (((1,), (1,)), ((), ())), preferred_element_...]
    pallas_call x0 -> x1, Pallas kernels: none -> 301 us  [fused(): pl.pallas_call(functools.partial(lstm_kernel, steps, rows), out_shape=(ja...]
    all_gather x3 -> x0, waiting for transfers between devices: 208 us -> none  [the longest x1 187 us: per_device(): lax.all_gather(w_rec, ('dp', 'fsdp'), axis=0, tiled=True)]
    psum x1 -> x0, blocking collectives: 40.1 us -> none  [per_device(): lax.psum((sums[3], sums[4], sums[5]), ('dp', 'fsdp'))]
    dynamic_update_slice x48 -> x0, other arithmetic: 31.9 us -> none  [the longest x36 21.8 us: lstm_forward(): state, saved = lax.scan(advance, start, (drives, keeps))]
    all_gather x1 -> x0, blocking collectives: 31.3 us -> none  [per_device(): lax.all_gather(bias_in, ('dp', 'fsdp'), axis=0, tiled=True)]
    psum x1 -> x0, waiting for transfers between devices: 28.1 us -> none  [per_device(): lax.psum((sums[3], sums[4], sums[5]), ('dp', 'fsdp'))]
  transfers between devices with their start and end apart: 7 -> 0, of which waited for: 6 -> 0; matrix products, arithmetic and copies ran while one was open for 15% -> 0% of each run, Pallas kernels for 0% -> 0%
where the time goes in v1:
time: 327 us; the launch traced here: 324 us
  Pallas kernels  301 us (92%)
  local copies, waits for them, and re-layouts  18.8 us (6%)
    pallas_call x1, Pallas kernels, fused(): pl.pallas_call(functools.partial(lstm_kernel, steps, rows), out_shape=(ja...  301 us
    unnamed x36, local copies, waits for them, and re-layouts  7.75 us

profile of v1, /device:TPU:13, one launch (start us, length us, event | category | flops | bytes accessed | tf_op | source)
XLA Modules:
  0.0 324.1 jit_solution(16587252283796656629)
XLA Ops:
  0.6 0.0 copy-start.5
  0.6 0.0 copy-start.8
  0.7 0.0 copy-start.9
  0.7 0.0 copy-start.10
  0.7 1.6 copy.29
  2.3 1.6 copy.32
  3.8 0.1 copy.23
  4.1 0.0 copy-start.1
  4.1 0.1 copy.24
  4.2 0.1 copy.25
  4.3 0.1 copy.26
  4.4 0.1 pad_add_fusion
  4.5 0.6 pad.38.ids_in
  5.2 0.0 copy-done.7
  5.2 0.0 copy-start.2
  5.2 0.6 pad.34.w_dec
  5.8 0.6 compare_reduce_fusion
  6.5 0.6 convert_select_fusion
  7.1 0.6 scatter.32.bias_dec
  7.7 0.0 copy-done.1
  7.7 301.3 %shard_map.152 = (f32[8,4,64,256]{3,2,1,0:T(8,128)}, f32[104,256]{1,0:T(8,128)}, f32[64,384]{1,0:T(8,128)}, bf16[2,6,32,2048]{3,2,1,0:T(8,128)(2,1)}, f32[112,384]{1,0:T(8,128)}) custom-call(bf16[8,4,64,256]{3,2,1,0:T(8,128)(2,1)} %bitcast.19, bf16[128,256]{1,0:T(8,128)(2,1)} %copy-done.2, bf16[64,384]{1,0:T(8,128)(2,1)} %pad.34.w_dec, ...), custom_call_target="tpu_custom_call" | custom-call | tf_op jit(solution)/shard_map/pallas_call | solution.py:807
  309.1 0.9 slice_bitcast_fusion
  310.0 0.8 copy.28
  310.8 1.3 slice_reduce_fusion
  312.1 1.2 slice.100
  313.9 1.3 slice.103
  315.2 2.8 copy.27
  318.0 2.5 copy.30
  320.5 1.1 copy.38
  321.7 0.6 copy.39
  322.3 0.0 copy-done.4
  322.3 0.6 copy.40
  (24 shorter events, 0.1 us)
Async XLA Ops:
  0.6 3.2 copy-start.5
  0.6 3.4 %copy-start.8 = (s32[2,32,6]{1,0,2:T(2,128)S(1)}, s32[2,32,6]{1,0,2:T(2,128)}, u32[]{:S(2)}) copy-start(s32[2,32,6]{1,0,2:T(2,128)} %param.19) | copy-start | bytes 4612
  0.7 3.5 %copy-start.9 = (s32[2,32,6]{1,0,2:T(2,128)S(1)}, s32[2,32,6]{1,0,2:T(2,128)}, u32[]{:S(2)}) copy-start(s32[2,32,6]{1,0,2:T(2,128)} %param.20) | copy-start | bytes 4612
  0.7 3.6 %copy-start.10 = (s32[2,32,6]{1,0,2:T(2,128)S(1)}, s32[2,32,6]{1,0,2:T(2,128)}, u32[]{:S(2)}) copy-start(s32[2,32,6]{1,0,2:T(2,128)} %param.21) | copy-start | bytes 4612
  0.7 4.4 %copy-start.6 = (bf16[100,256]{1,0:T(8,128)(2,1)S(1)}, bf16[100,256]{1,0:T(8,128)(2,1)}, u32[]{:S(2)}) copy-start(bf16[100,256]{1,0:T(8,128)(2,1)} %param.23) | copy-start | bytes 153604
  0.7 4.4 %copy-start.12 = (bf16[256]{0:T(256)(128)(2,1)S(1)}, bf16[256]{0:T(256)(128)(2,1)}, u32[]{:S(2)}) copy-start(bf16[256]{0:T(256)(128)(2,1)} %param.24) | copy-start | bytes 1540
  0.7 4.5 %copy-start.7 = (bf16[64,275]{1,0:T(8,128)(2,1)S(1)}, bf16[64,275]{1,0:T(8,128)(2,1)}, u32[]{:S(2)}) copy-start(bf16[64,275]{1,0:T(8,128)(2,1)} %param.26) | copy-start | bytes 105604
  0.7 5.7 %copy-start.11 = (bf16[275]{0:T(512)(128)(2,1)S(1)}, bf16[275]{0:T(512)(128)(2,1)}, u32[]{:S(2)}) copy-start(bf16[275]{0:T(512)(128)(2,1)} %param.27) | copy-start | bytes 1654
  4.1 3.7 %copy-start.1 = (bf16[128,384]{1,0:T(8,128)(2,1)}, bf16[128,384]{1,0:T(8,128)(2,1)S(1)}, u32[]{:S(2)}) copy-start(bf16[128,384]{1,0:T(8,128)(2,1)S(1)} %scatter.30.emb_t) | copy-start | bytes 294916
  5.2 2.6 copy-start.2
  318.0 2.5 copy-start
  320.5 1.2 copy-start.3
  320.5 1.8 copy-start.4
